TPU v7x, 32 devices: a whole 2x2x4 slice. The times are simulated.
32 devices in a mesh: grp: 4 (over y, x), sub: 8 (over z, core).
Axes of the slice: x: 2, y: 2, z: 4, core: 2. Of those that a mesh axis runs over, the one named last changes fastest.
Arguments:
- neumann: bfloat16 [4, 8, 1024, 1024], P('grp', 'sub'), may hold values from -1 to 4
- dirichlet: bfloat16 [4, 8, 1024, 1024], P('grp', 'sub'), may hold values from -1 to 4
- coarse_inverse: float32 [4, 8, 128, 256], P('grp', 'sub'), may hold values from -1 to 3
- loads: bfloat16 [4, 8, 1024, 256], P('grp', 'sub'), may hold values from -72 to 72
- iface_sizes: int32 [4, 8], P('grp', 'sub'), may hold values from 1 to 512, 2048 in all within a row
- wave_dirs: int32 [4, 8, 32], P('grp', 'sub'), may hold values from 0 to 63
Outputs:
- dual: float32 [4, 8, 512, 256], P('grp', 'sub')
- residual: float32 [4, 8, 512, 256], P('grp', 'sub')
Inputs may be any that keep to these rules, and one draw needn't show every extreme that they name: `iface_sizes`: the 8 sizes of one group sum to 2048, and in each group one size is exactly 512.
All inputs are finite; a program needn't handle non-finite values.
Results may differ from a plain program's by a relative error of at most 0.005.
Values may be sent and summed in bfloat16 or wider, within the bound.
A program may use at most 64 MiB of HBM per device.

v0:
```python
import jax
import jax.numpy as jnp
from jax import lax
from jax.sharding import PartitionSpec as P

NDIR = 64
ITERS = 2


wave_number = 0.785
highest = lax.Precision.HIGHEST


def passed_along(block, axis, distance):
    devices = range(lax.axis_size(axis))
    route = [((i - distance) % len(devices), i) for i in devices]
    return lax.ppermute(block, axis, route)


def local_waves(size_here, directions, reach):
    rows = jnp.arange(reach).astype(jnp.float32)
    live = (jnp.arange(reach) < size_here).astype(jnp.float32)
    angle = 2.0 * jnp.pi * directions.astype(jnp.float32) / NDIR
    phase = (jnp.arange(directions.shape[0]) % 2).astype(jnp.float32) * (jnp.pi / 2.0)
    basis = jnp.cos(wave_number * rows[:, None] * jnp.cos(angle)[None, :] + phase[None, :])
    return (basis * live[:, None] / jnp.sqrt(jnp.float32(reach)), live)


def shards(neumann, dirichlet, coarse_inverse, loads, iface_sizes, wave_dirs):
    neumann_mat = neumann[0, 0]
    dirichlet_mat = dirichlet[0, 0]
    tile = coarse_inverse[0, 0]
    width = neumann_mat.shape[0]
    reach = width // 2
    columns = loads.shape[3]
    basis, live = local_waves(iface_sizes[0, 0], wave_dirs[0, 0], reach)
    groups = lax.axis_size("grp")

    def spread_local(values):
        left = passed_along(values, "sub", 1)
        middle = jnp.zeros((width - 2 * reach, columns), jnp.bfloat16)
        return jnp.concatenate([-left, middle, jnp.flip(values, 0)], axis=0)

    def jump_local(product):
        next_head = passed_along(product[:reach], "sub", -1)
        return (jnp.flip(product[width - reach :], 0) - next_head) * live[:, None]

    def apply_local(matrix, values):
        vector = spread_local(values.astype(jnp.bfloat16))
        return jump_local(jnp.dot(matrix, vector, preferred_element_type=jnp.float32))

    def coefficients(values):
        return jnp.dot(basis.T, values, precision=highest)

    def coarse_solve(values):
        gathered = lax.all_gather(coefficients(values), "sub", axis=0, tiled=True)
        return lax.psum_scatter(
            jnp.dot(tile, gathered, precision=highest), "grp", scatter_dimension=0, tiled=True
        )

    def coarse_with_stat(values, partial_value):
        gathered, stats = (
            lax.all_gather(coefficients(values), "sub", axis=0, tiled=True),
            lax.all_gather(partial_value[None, :], "sub", axis=0, tiled=True),
        )
        group_stat = jnp.sum(stats, axis=0)
        term = jnp.dot(tile, gathered, precision=highest)
        copies = jnp.broadcast_to(group_stat[None, :], (groups, columns))
        solved, totals = (
            lax.psum_scatter(term, "grp", scatter_dimension=0, tiled=True),
            lax.psum_scatter(copies, "grp", scatter_dimension=0, tiled=True),
        )
        return (solved, totals[0])

    def lift(solved):
        return jnp.dot(basis, solved, precision=highest)

    dual_rhs = jump_local(jnp.dot(neumann_mat, loads[0, 0], preferred_element_type=jnp.float32))
    dual = lift(coarse_solve(dual_rhs))
    residual = dual_rhs - apply_local(neumann_mat, dual)
    direction = dual_rhs
    rho_prev = jnp.ones((columns,), jnp.float32)
    coarse_res = coarse_solve(residual)
    for step in range(ITERS):
        projected = residual - lift(coarse_res)
        precond = apply_local(dirichlet_mat, projected)
        coarse_pre, rho = coarse_with_stat(precond, jnp.sum(projected * precond, axis=0))
        search = precond - lift(coarse_pre)
        if step == 0:
            direction = search
        else:
            direction = search + rho / rho_prev * direction
        image = apply_local(neumann_mat, direction)
        if step + 1 < ITERS:
            coarse_img, curvature = coarse_with_stat(image, jnp.sum(direction * image, axis=0))
            alpha = rho / curvature
            coarse_res = coarse_res - alpha * coarse_img
        else:
            alpha = rho / lax.psum(jnp.sum(direction * image, axis=0), ("grp", "sub"))
        dual = dual + alpha * direction
        residual = residual - alpha * image
        rho_prev = rho
    return (dual[None, None], residual[None, None])


def solution(mesh):
    return jax.shard_map(
        shards,
        mesh=mesh,
        in_specs=(
            P("grp", "sub", None, None),
            P("grp", "sub", None, None),
            P("grp", "sub", None, None),
            P("grp", "sub", None, None),
            P("grp", "sub"),
            P("grp", "sub", None),
        ),
        out_specs=(P("grp", "sub", None, None), P("grp", "sub", None, None)),
        check_vma=False,
    )
```

profile of v0, /device:TPU:0, one launch (start us, length us, event | category | flops | bytes accessed | tf_op | source)
XLA Modules:
  0.0 395.2 jit_solution(8021162017483263785)
XLA Ops:
  11.6 4.5 %collective-permute-start = (f32[512,256]{1,0:T(8,128)}, f32[512,256]{1,0:T(8,128)S(1)}, u32[]{:S(2)}, u32[]{:S(2)}) collective-permute-start(f32[512,256]{1,0:T(8,128)} %get-tuple-element.22), channel_id=1, source_target_pairs={{1,0},{2,1},{3,2},{4,3},{5,4},{6,5},{7,6},{0,7},{9,8},{10,9},{11,1... | collective-permute-start | bytes 1572872 | tf_op jit(solution)/shard_map/ppermute | solution.py:17
  16.7 3.4 rev.35
  20.2 2.8 collective-permute-done
  24.6 14.4 %all_gather.24 = f32[256,256]{1,0:T(8,128)S(1)} all-gather(f32[32,256]{1,0:T(8,128)S(1)} %fusion.49), channel_id=1, replica_groups=mesh['grp'=4,'sub'=8] {'sub'}, dimensions={0}, use_global_device_ids=true | all-gather | bytes 294912 | tf_op jit(solution)/shard_map/all_gather | solution.py:56
  40.5 22.4 %reduce-scatter.16.cloned.1.call-done = f32[32,256]{1,0:T(8,128)} async-done(((f32[128,256]{1,0:T(8,128)}), f32[32,256]{1,0:T(8,128)}) %reduce-scatter.16.cloned.1.call-update) | async-done | bytes 32784
  62.8 3.0 fusion.133
  68.4 5.1 %collective-permute-done.1 = bf16[512,256]{1,0:T(8,128)(2,1)} collective-permute-done((bf16[512,256]{1,0:T(8,128)(2,1)S(1)}, bf16[512,256]{1,0:T(8,128)(2,1)}, u32[]{:S(2)}, u32[]{:S(2)}) %collective-permute-start.1) | collective-permute-done | bytes 262176 | tf_op jit(solution)/shard_map/ppermute | solution.py:17
  77.2 4.8 %rev.37 = f32[512,256]{1,0:T(8,128)} reverse(f32[512,256]{1,0:T(8,128)} %get-tuple-element.21), dimensions={0} | reverse | bytes 1048576 | tf_op jit(solution)/shard_map/jit(_flip)/rev | solution.py:46
  87.3 14.5 %all_gather.25 = f32[256,256]{1,0:T(8,128)S(1)} all-gather(f32[32,256]{1,0:T(8,128)S(1)} %fusion.47), channel_id=1, replica_groups=mesh['grp'=4,'sub'=8] {'sub'}, dimensions={0}, use_global_device_ids=true | all-gather | bytes 294912 | tf_op jit(solution)/shard_map/all_gather | solution.py:56
  103.2 22.1 %reduce-scatter.18.cloned.1.call-done = f32[32,256]{1,0:T(8,128)} async-done(((f32[128,256]{1,0:T(8,128)}), f32[32,256]{1,0:T(8,128)}) %reduce-scatter.18.cloned.1.call-update) | async-done | bytes 32784
  125.3 3.0 fusion.134
  128.6 7.3 %collective-permute-done.3 = bf16[512,256]{1,0:T(8,128)(2,1)S(1)} collective-permute-done((bf16[512,256]{1,0:T(8,128)(2,1)S(1)}, bf16[512,256]{1,0:T(8,128)(2,1)S(1)}, u32[]{:S(2)}, u32[]{:S(2)}) %collective-permute-start.3) | collective-permute-done | bytes 262176 | tf_op jit(solution)/shard_map/ppermute | solution.py:17
  141.8 4.4 %collective-permute-done.4 = f32[512,256]{1,0:T(8,128)} collective-permute-done((f32[512,256]{1,0:T(8,128)}, f32[512,256]{1,0:T(8,128)}, u32[]{:S(2)}, u32[]{:S(2)}) %collective-permute-start.4) | collective-permute-done | bytes 524320 | tf_op jit(solution)/shard_map/ppermute | solution.py:17
  149.7 14.5 %all_gather.27 = f32[256,256]{1,0:T(8,128)S(1)} all-gather(f32[32,256]{1,0:T(8,128)S(1)} %fusion.46), channel_id=1, replica_groups=mesh['grp'=4,'sub'=8] {'sub'}, dimensions={0}, use_global_device_ids=true | all-gather | bytes 294912 | tf_op jit(solution)/shard_map/all_gather | solution.py:63
  165.6 22.1 %reduce-scatter.20.cloned.1.call-done = f32[32,256]{1,0:T(8,128)} async-done(((f32[128,256]{1,0:T(8,128)}), f32[32,256]{1,0:T(8,128)}) %reduce-scatter.20.cloned.1.call-update) | async-done | bytes 32784
  192.8 5.1 %collective-permute-done.5 = bf16[512,256]{1,0:T(8,128)(2,1)} collective-permute-done((bf16[512,256]{1,0:T(8,128)(2,1)S(1)}, bf16[512,256]{1,0:T(8,128)(2,1)}, u32[]{:S(2)}, u32[]{:S(2)}) %collective-permute-start.5) | collective-permute-done | bytes 262176 | tf_op jit(solution)/shard_map/ppermute | solution.py:17
  201.6 4.8 %rev.41 = f32[512,256]{1,0:T(8,128)} reverse(f32[512,256]{1,0:T(8,128)} %get-tuple-element.17), dimensions={0} | reverse | bytes 1048576 | tf_op jit(solution)/shard_map/jit(_flip)/rev | solution.py:46
  212.2 14.5 %all_gather.29 = f32[256,256]{1,0:T(8,128)S(1)} all-gather(f32[32,256]{1,0:T(8,128)S(1)} %fusion.45), channel_id=1, replica_groups=mesh['grp'=4,'sub'=8] {'sub'}, dimensions={0}, use_global_device_ids=true | all-gather | bytes 294912 | tf_op jit(solution)/shard_map/all_gather | solution.py:63
  229.5 9.9 %all-gather.3 = f32[8,1,256]{2,1,0:T(1,128)S(1)} all-gather(f32[1,1,256]{2,1,0:T(1,128)S(1)} %bitcast.93), channel_id=2, replica_groups=mesh['grp'=4,'sub'=8] {'sub'}, dimensions={0}, use_global_device_ids=true | all-gather | bytes 9216 | tf_op jit(solution)/shard_map/all_gather | solution.py:64
  239.4 8.9 %all-gather.4 = f32[8,1,256]{2,1,0:T(1,128)S(1)} all-gather(f32[1,1,256]{2,1,0:T(1,128)S(1)} %bitcast.94), channel_id=3, replica_groups=mesh['grp'=4,'sub'=8] {'sub'}, dimensions={0}, use_global_device_ids=true | all-gather | bytes 9216 | tf_op jit(solution)/shard_map/all_gather | solution.py:64
  248.3 9.1 %all-reduce.3 = (f32[4,256]{1,0:T(4,128)S(1)}, f32[4,256]{1,0:T(4,128)S(1)}) all-reduce(f32[4,256]{1,0:T(4,128)S(1)} %broadcast_in_dim.19, f32[4,256]{1,0:T(4,128)S(1)} %broadcast_in_dim.17), channel_id=9, replica_groups=mesh['grp'=4,'sub'=8] {'grp'}, use_global_device_ids=true, to_apply=%region_8.9.clone | all-reduce | flops 2048 | bytes 16384
  260.1 3.4 fusion.136
  266.1 5.1 %collective-permute-done.7 = bf16[512,256]{1,0:T(8,128)(2,1)} collective-permute-done((bf16[512,256]{1,0:T(8,128)(2,1)S(1)}, bf16[512,256]{1,0:T(8,128)(2,1)}, u32[]{:S(2)}, u32[]{:S(2)}) %collective-permute-start.7) | collective-permute-done | bytes 262176 | tf_op jit(solution)/shard_map/ppermute | solution.py:17
  275.6 4.8 %rev.43 = f32[512,256]{1,0:T(8,128)} reverse(f32[512,256]{1,0:T(8,128)} %get-tuple-element.15), dimensions={0} | reverse | bytes 1048576 | tf_op jit(solution)/shard_map/jit(_flip)/rev | solution.py:46
  286.3 14.5 %all_gather.31 = f32[256,256]{1,0:T(8,128)S(1)} all-gather(f32[32,256]{1,0:T(8,128)S(1)} %fusion.44), channel_id=1, replica_groups=mesh['grp'=4,'sub'=8] {'sub'}, dimensions={0}, use_global_device_ids=true | all-gather | bytes 294912 | tf_op jit(solution)/shard_map/all_gather | solution.py:63
  302.2 9.2 %all-gather.5 = f32[8,1,256]{2,1,0:T(1,128)S(1)} all-gather(f32[1,1,256]{2,1,0:T(1,128)S(1)} %bitcast.95), channel_id=4, replica_groups=mesh['grp'=4,'sub'=8] {'sub'}, dimensions={0}, use_global_device_ids=true | all-gather | bytes 9216 | tf_op jit(solution)/shard_map/all_gather | solution.py:64
  311.4 8.9 %all-reduce.2 = f32[4,256]{1,0:T(4,128)S(1)} all-reduce(f32[4,256]{1,0:T(4,128)S(1)} %broadcast_in_dim.21), channel_id=11, replica_groups=mesh['grp'=4,'sub'=8] {'grp'}, use_global_device_ids=true, to_apply=%region_12.13.clone | all-reduce | flops 1024 | bytes 8192
  323.6 3.3 fusion.137
  329.5 5.1 %collective-permute-done.9 = bf16[512,256]{1,0:T(8,128)(2,1)} collective-permute-done((bf16[512,256]{1,0:T(8,128)(2,1)S(1)}, bf16[512,256]{1,0:T(8,128)(2,1)}, u32[]{:S(2)}, u32[]{:S(2)}) %collective-permute-start.9) | collective-permute-done | bytes 262176 | tf_op jit(solution)/shard_map/ppermute | solution.py:17
  338.3 4.8 %rev.45 = f32[512,256]{1,0:T(8,128)} reverse(f32[512,256]{1,0:T(8,128)} %get-tuple-element.13), dimensions={0} | reverse | bytes 1048576 | tf_op jit(solution)/shard_map/jit(_flip)/rev | solution.py:46
  346.8 38.9 %psum.7 = f32[256]{0:T(256)S(1)} all-reduce(f32[256]{0:T(256)S(1)} %multiply_reduce_fusion), channel_id=1, replica_groups=mesh['grp'=4,'sub'=8] {'grp','sub'}, use_global_device_ids=true, to_apply=%region_15.16 | all-reduce | flops 256 | bytes 2048 | tf_op jit(solution)/shard_map/psum | solution.py:99
  385.7 2.9 subtract_bitcast_fusion
  (110 shorter events, 79.2 us)
Async XLA Ops:
  7.2 1.6 copy-start
  7.2 55.6 %reduce-scatter.16.cloned.1.call-start = ((), (), s32[]{:S(2)}) async-start(), calls=%async_computation.5 | async-start | bytes 163840
  10.5 9.7 %copy-start.10 = (s32[1,1,32]{2,1,0:T(1,128)S(1)}, s32[1,1,32]{2,1,0:T(1,128)}, u32[]{:S(2)}) copy-start(s32[1,1,32]{2,1,0:T(1,128)} %param.11) | copy-start | bytes 388
  10.5 28.5 %copy-start.4 = (f32[1,1,128,256]{3,2,1,0:T(8,128)S(1)}, f32[1,1,128,256]{3,2,1,0:T(8,128)}, u32[]{:S(2)}) copy-start(f32[1,1,128,256]{3,2,1,0:T(8,128)} %param.8) | copy-start | bytes 393220
  11.6 11.5 %collective-permute-start = (f32[512,256]{1,0:T(8,128)}, f32[512,256]{1,0:T(8,128)S(1)}, u32[]{:S(2)}, u32[]{:S(2)}) collective-permute-start(f32[512,256]{1,0:T(8,128)} %get-tuple-element.22), channel_id=1, source_target_pairs={{1,0},{2,1},{3,2},{4,3},{5,4},{6,5},{7,6},{0,7},{9,8},{10,9},{11,1... | collective-permute-start | bytes 1572872 | tf_op jit(solution)/shard_map/ppermute | solution.py:17
  23.1 53.1 %copy-start.5 = (f32[512,256]{1,0:T(8,128)}, f32[512,256]{1,0:T(8,128)S(1)}, u32[]{:S(2)}) copy-start(f32[512,256]{1,0:T(8,128)S(1)} %collective-permute-done) | copy-start | bytes 1572868
  40.4 84.9 %reduce-scatter.18.cloned.1.call-start = ((), (), s32[]{:S(2)}) async-start(), calls=%async_computation.6 | async-start | bytes 163840
  65.8 7.7 %collective-permute-start.1 = (bf16[512,256]{1,0:T(8,128)(2,1)S(1)}, bf16[512,256]{1,0:T(8,128)(2,1)}, u32[]{:S(2)}, u32[]{:S(2)}) collective-permute-start(bf16[512,256]{1,0:T(8,128)(2,1)S(1)} %get-tuple-element.26), channel_id=1, source_target_pairs={{7,0},{0,1},{1,2},{2,3},{3,4},{4,5},{5,6},{6,7},{15,8},{8,9},{9,10... | collective-permute-start | bytes 786440 | tf_op jit(solution)/shard_map/ppermute | solution.py:17
  77.2 7.0 %collective-permute-start.2 = (f32[512,256]{1,0:T(8,128)}, f32[512,256]{1,0:T(8,128)}, u32[]{:S(2)}, u32[]{:S(2)}) collective-permute-start(f32[512,256]{1,0:T(8,128)} %get-tuple-element.20), channel_id=1, source_target_pairs={{1,0},{2,1},{3,2},{4,3},{5,4},{6,5},{7,6},{0,7},{9,8},{10,9},{11,1... | collective-permute-start | bytes 1572872 | tf_op jit(solution)/shard_map/ppermute | solution.py:17
  103.2 84.5 %reduce-scatter.20.cloned.1.call-start = ((), (), s32[]{:S(2)}) async-start(), calls=%async_computation.7 | async-start | bytes 163840
  128.3 7.6 %collective-permute-start.3 = (bf16[512,256]{1,0:T(8,128)(2,1)S(1)}, bf16[512,256]{1,0:T(8,128)(2,1)S(1)}, u32[]{:S(2)}, u32[]{:S(2)}) collective-permute-start(bf16[512,256]{1,0:T(8,128)(2,1)S(1)} %get-tuple-element.28), channel_id=1, source_target_pairs={{7,0},{0,1},{1,2},{2,3},{3,4},{4,5},{5,6},{6,7},{15,8},{8,9},{9,10... | collective-permute-start | bytes 786440 | tf_op jit(solution)/shard_map/ppermute | solution.py:17
  139.2 7.0 %collective-permute-start.4 = (f32[512,256]{1,0:T(8,128)}, f32[512,256]{1,0:T(8,128)}, u32[]{:S(2)}, u32[]{:S(2)}) collective-permute-start(f32[512,256]{1,0:T(8,128)} %get-tuple-element.18), channel_id=1, source_target_pairs={{1,0},{2,1},{3,2},{4,3},{5,4},{6,5},{7,6},{0,7},{9,8},{10,9},{11,1... | collective-permute-start | bytes 1572872 | tf_op jit(solution)/shard_map/ppermute | solution.py:17
  148.2 17.3 %copy-start.3 = (f32[512,256]{1,0:T(8,128)}, f32[512,256]{1,0:T(8,128)S(1)}, u32[]{:S(2)}) copy-start(f32[512,256]{1,0:T(8,128)S(1)} %get-tuple-element.9) | copy-start | bytes 1572868
  165.5 93.1 %reduce-scatter.22.cloned.1.call-start = ((), (), s32[]{:S(2)}) async-start(), calls=%async_computation.8 | async-start | bytes 163840
  190.2 7.8 %collective-permute-start.5 = (bf16[512,256]{1,0:T(8,128)(2,1)S(1)}, bf16[512,256]{1,0:T(8,128)(2,1)}, u32[]{:S(2)}, u32[]{:S(2)}) collective-permute-start(bf16[512,256]{1,0:T(8,128)(2,1)S(1)} %get-tuple-element.30), channel_id=1, source_target_pairs={{7,0},{0,1},{1,2},{2,3},{3,4},{4,5},{5,6},{6,7},{15,8},{8,9},{9,10... | collective-permute-start | bytes 786440 | tf_op jit(solution)/shard_map/ppermute | solution.py:17
  201.6 7.0 %collective-permute-start.6 = (f32[512,256]{1,0:T(8,128)}, f32[512,256]{1,0:T(8,128)}, u32[]{:S(2)}, u32[]{:S(2)}) collective-permute-start(f32[512,256]{1,0:T(8,128)} %get-tuple-element.16), channel_id=1, source_target_pairs={{1,0},{2,1},{3,2},{4,3},{5,4},{6,5},{7,6},{0,7},{9,8},{10,9},{11,1... | collective-permute-start | bytes 1572872 | tf_op jit(solution)/shard_map/ppermute | solution.py:17
  206.4 21.7 %copy-start.11 = (u32[32]{0:T(128)S(1)}, u32[32]{0:T(128)}, u32[]{:S(2)}) copy-start(u32[32]{0:T(128)} %constant.38) | copy-start | bytes 388
  206.4 22.3 %copy-start.6 = (f32[32,256]{1,0:T(8,128)S(1)}, f32[32,256]{1,0:T(8,128)}, u32[]{:S(2)}) copy-start(f32[32,256]{1,0:T(8,128)} %reduce-scatter.18.cloned.1.call-done) | copy-start | bytes 98308
  206.4 23.1 %copy-start.8 = (f32[256]{0:T(256)S(1)}, f32[256]{0:T(256)}, u32[]{:S(2)}) copy-start(f32[256]{0:T(256)} %get-tuple-element.8) | copy-start | bytes 3076
  210.0 0.8 copy-start.1
  228.1 95.5 %reduce-scatter.24.cloned.1.call-start = ((), (), s32[]{:S(2)}) async-start(), calls=%async_computation.9 | async-start | bytes 163840
  257.4 2.7 copy-start.9
  263.5 7.7 %collective-permute-start.7 = (bf16[512,256]{1,0:T(8,128)(2,1)S(1)}, bf16[512,256]{1,0:T(8,128)(2,1)}, u32[]{:S(2)}, u32[]{:S(2)}) collective-permute-start(bf16[512,256]{1,0:T(8,128)(2,1)S(1)} %get-tuple-element.32), channel_id=1, source_target_pairs={{7,0},{0,1},{1,2},{2,3},{3,4},{4,5},{5,6},{6,7},{15,8},{8,9},{9,10... | collective-permute-start | bytes 786440 | tf_op jit(solution)/shard_map/ppermute | solution.py:17
  275.6 7.0 %collective-permute-start.8 = (f32[512,256]{1,0:T(8,128)}, f32[512,256]{1,0:T(8,128)}, u32[]{:S(2)}, u32[]{:S(2)}) collective-permute-start(f32[512,256]{1,0:T(8,128)} %get-tuple-element.14), channel_id=1, source_target_pairs={{1,0},{2,1},{3,2},{4,3},{5,4},{6,5},{7,6},{0,7},{9,8},{10,9},{11,1... | collective-permute-start | bytes 1572872 | tf_op jit(solution)/shard_map/ppermute | solution.py:17
  284.1 0.8 copy-start.2
  326.9 7.7 %collective-permute-start.9 = (bf16[512,256]{1,0:T(8,128)(2,1)S(1)}, bf16[512,256]{1,0:T(8,128)(2,1)}, u32[]{:S(2)}, u32[]{:S(2)}) collective-permute-start(bf16[512,256]{1,0:T(8,128)(2,1)S(1)} %get-tuple-element.34), channel_id=1, source_target_pairs={{7,0},{0,1},{1,2},{2,3},{3,4},{4,5},{5,6},{6,7},{15,8},{8,9},{9,10... | collective-permute-start | bytes 786440 | tf_op jit(solution)/shard_map/ppermute | solution.py:17
  337.2 48.5 %copy-start.7 = (f32[1,256]{1,0:T(1,128)S(1)}, f32[1,256]{1,0:T(1,128)}, u32[]{:S(2)}) copy-start(f32[1,256]{1,0:T(1,128)} %dynamic-slice_divide_fusion) | copy-start | bytes 3076
  338.3 7.0 %collective-permute-start.10 = (f32[512,256]{1,0:T(8,128)}, f32[512,256]{1,0:T(8,128)}, u32[]{:S(2)}, u32[]{:S(2)}) collective-permute-start(f32[512,256]{1,0:T(8,128)} %get-tuple-element.12), channel_id=1, source_target_pairs={{1,0},{2,1},{3,2},{4,3},{5,4},{6,5},{7,6},{0,7},{9,8},{10,9},{11,1... | collective-permute-start | bytes 1572872 | tf_op jit(solution)/shard_map/ppermute | solution.py:17
Sparse Core Ops, SparseCore 0:
  40.5 22.2 reduce-scatter.15
  103.3 21.9 reduce-scatter.17
  165.6 22.0 reduce-scatter.19
  228.2 21.9 reduce-scatter.21
  302.3 21.2 reduce-scatter.23
where the time goes:
time: 398 us; the launch traced here: 395 us
  blocking collectives  157 us (39%)
  waiting for transfers between devices  113 us (28%)
  local copies, waits for them, and re-layouts  51.6 us (13%)
  matrix products  36.7 us (9%)
  other arithmetic  17.6 us (4%)
  between operations  14.7 us (4%)
  starting transfers between devices  4.78 us (1%)
    unnamed x10, waiting for transfers between devices  68.7 us
    ppermute x11, waiting for transfers between devices, passed_along(): return lax.ppermute(block, axis, route)  43.9 us
    all_gather x3, blocking collectives, coarse_with_stat(): lax.all_gather(coefficients(values), 'sub', axis=0, tiled=True)  43.5 us
    psum x1, blocking collectives, shards(): alpha = rho / lax.psum(jnp.sum(direction * image, axis=0), ('grp', 'sub'))  38.9 us
    all_gather x2, blocking collectives, coarse_solve(): gathered = lax.all_gather(coefficients(values), 'sub', axis=0, tiled=True)  28.9 us
    all_gather x3, blocking collectives, coarse_with_stat(): lax.all_gather(partial_value[None, :], 'sub', axis=0, tiled=True)  28 us
    rev x6, local copies, waits for them, and re-layouts, jump_local(): return (jnp.flip(product[width - reach:], 0) - next_head) * live[:, None]  25.1 us
    unnamed x2, blocking collectives  17.9 us
  transfers between devices with their start and end apart: 16, of which 15 were waited for; matrix products, arithmetic and copies ran while one was open for 10% of the time, Pallas kernels for 0%

commit v1 on v0

v1 whole, which is shorter than its diff:
```python
import functools

import jax
import jax.numpy as jnp
from jax import lax
from jax.experimental import pallas as pl
from jax.experimental.pallas import tpu as pltpu
from jax.sharding import PartitionSpec as P

NDIR = 64
ITERS = 2
WAVE_NUMBER = 0.785
STAT = 8
MESH = pl.DeviceIdType.MESH
f32, bf16 = jnp.float32, jnp.bfloat16


def dot(a, b):
    return jnp.dot(a, b, preferred_element_type=f32)


def split(values):
    high = values.astype(bf16)
    return high, (values - high.astype(f32)).astype(bf16)


def kernel(
    groups, members, size_ref, dirs_ref, neumann, dirichlet_hbm, loads, tile,
    dual_ref, res_ref,
    dirichlet, n_left, n_right, d_left, d_right, n_send, d_send,
    u_send, u_recv, tile_nb, tile_hi, tile_lo, bases, wave_cat, wave_t,
    gath, stage, red, r_send, r_recv,
    res3, dir3, vec, x_left, x_right,
    load_sem, set_send, set_recv, g_send, f_send, g_recv, red_send, red_recv, r_ssem, r_rsem,
):
    reach = n_left.shape[0]
    columns = loads.shape[1]
    waves = dirs_ref.shape[1]
    span = 3 * waves
    half = members // 2
    g, s = lax.axis_index("grp"), lax.axis_index("sub")
    nxt, prv = lax.rem(s + 1, members), lax.rem(s + members - 1, members)
    partner = s + 1 - 2 * lax.rem(s, 2)

    def remote(src, dst, send, recv, to):
        return pltpu.make_async_remote_copy(
            src_ref=src, dst_ref=dst, send_sem=send, recv_sem=recv, device_id=to, device_id_type=MESH
        )

    load_d = pltpu.make_async_copy(dirichlet_hbm, dirichlet, load_sem)
    load_d.start()

    barrier = pltpu.get_barrier_semaphore()

    def greet_sub(k, carry):
        pl.semaphore_signal(barrier, inc=1, device_id=(g, lax.rem(s + k, members)), device_id_type=MESH)
        return carry

    lax.fori_loop(1, members, greet_sub, 0)
    for k in range(1, groups):
        pl.semaphore_signal(barrier, inc=1, device_id=(lax.rem(g + k, groups), s), device_id_type=MESH)

    u_send[...] = dot(neumann[:reach, :], loads[...])
    pl.semaphore_wait(barrier, members - 1 + groups - 1)
    send_u = remote(u_send, u_recv, set_send.at[0], set_recv.at[0], (g, prv))
    send_u.start()
    send_t = [
        remote(tile, tile_nb.at[0], set_send.at[1], set_recv.at[1], (g, nxt)),
        remote(tile, tile_nb.at[1], set_send.at[2], set_recv.at[2], (g, prv)),
    ]

    back = (
        lax.broadcasted_iota(jnp.int32, (reach, reach), 0) + lax.broadcasted_iota(jnp.int32, (reach, reach), 1)
        == reach - 1
    )
    flip = jnp.where(back, 1.0, 0.0).astype(bf16)

    def prepare(matrix, left, outgoing):
        outgoing[:, :reach] = matrix[:reach, :reach]
        outgoing[:, reach:] = dot(matrix[:reach, reach:], flip).astype(bf16)
        left[...] = dot(flip, matrix[reach:, :]).astype(bf16)

    prepare(neumann, n_left, n_send)
    v = dot(n_left[...], loads[...])
    vec[...] = v
    n_left[:, reach:] = dot(n_left[:, reach:], flip).astype(bf16)

    size = size_ref[0, 0]
    rows = lax.broadcasted_iota(jnp.int32, (waves, reach), 1)
    same = (
        lax.broadcasted_iota(jnp.int32, (waves, waves), 0) == lax.broadcasted_iota(jnp.int32, (waves, waves), 1)
    )
    dirs = jnp.sum(jnp.where(same, dirs_ref[...].astype(f32), 0.0), axis=1, keepdims=True)
    angle = 2.0 * jnp.pi * dirs / NDIR
    odd = lax.rem(lax.broadcasted_iota(jnp.int32, (waves, 1), 0), 2).astype(f32)
    basis = jnp.cos(WAVE_NUMBER * rows.astype(f32) * jnp.cos(angle) + odd * (jnp.pi / 2.0))
    basis = jnp.where(rows < size, basis, 0.0) / jnp.sqrt(f32(reach))
    high, low = split(basis)
    wave_t[:waves, :] = high
    wave_t[waves:, :] = low
    bases[1] = basis

    def stack_waves(k):
        hi, lo = split(bases[k])
        fill = jnp.zeros((wave_cat.shape[2] - span, reach), f32)
        padded = jnp.concatenate([hi.astype(f32), lo.astype(f32), hi.astype(f32), fill], axis=0)
        wave_cat[k] = padded.T.astype(bf16)

    send_w = [
        remote(bases.at[1], bases.at[0], set_send.at[3], set_recv.at[3], (g, nxt)),
        remote(bases.at[1], bases.at[2], set_send.at[4], set_recv.at[4], (g, prv)),
    ]
    send_n = remote(n_send, n_right, set_send.at[5], set_recv.at[5], (g, prv))
    send_d = remote(d_send, d_right, set_send.at[6], set_recv.at[6], (g, prv))
    send_u.wait_send()
    for copy in send_t + send_w + [send_n]:
        copy.start()

    live = lax.broadcasted_iota(jnp.int32, (reach, columns), 0) < size
    send_u.wait_recv()
    rhs = jnp.where(live, vec[...] - u_recv[...], 0.0)
    res3[1] = rhs

    def lift(k, coarse):
        hi, lo = split(coarse)
        fill = jnp.zeros((wave_cat.shape[2] - span, columns), bf16)
        return dot(wave_cat[k], jnp.concatenate([hi, hi, lo, fill], axis=0))

    def product(left, right):
        return jnp.where(live, dot(left[...], x_left[...]) + dot(right[...], x_right[...]), 0.0)

    def set_x(k, values):
        if k == 0:
            x_left[:reach, :] = (-values).astype(bf16)
        elif k == 1:
            own = values.astype(bf16)
            x_left[reach:, :] = own
            x_right[:reach, :] = own
        else:
            x_right[reach:, :] = (-values).astype(bf16)

    def fold(values):
        return jnp.sum(values.reshape(reach // STAT, STAT, columns), axis=0)

    def exchange(slot, lo, count, hook=None):
        part = pl.ds(lo, count)

        def block(owner):
            return gath.at[slot, owner, part]

        def send_peer(k):
            to = lax.rem(s + 2 * k, members)
            return remote(block(s), block(s), g_send.at[slot, k], g_recv.at[slot, s], (g, to))

        def relay(k):
            src = lax.rem(s + members - 2 * k, members)
            return remote(block(src), block(src), f_send.at[slot, k], g_recv.at[slot, src], (g, partner))

        def arrival(k):
            src = lax.rem(partner + members - 2 * k, members)
            return remote(block(src), block(src), f_send.at[slot, k], g_recv.at[slot, src], (g, partner))

        def loop(low, body):
            def step(k, carry):
                body(k)
                return carry

            lax.fori_loop(low, half, step, 0, unroll=half <= 8)

        loop(1, lambda k: send_peer(k).start())
        relay(0).start()
        if hook is not None:
            hook()

        def pass_on(k):
            relay(k).wait_recv()
            relay(k).start()

        loop(1, pass_on)
        loop(0, lambda k: arrival(k).wait_recv())
        loop(1, lambda k: send_peer(k).wait_send())
        loop(0, lambda k: relay(k).wait_send())

    def reduce_groups(slot, lo, count):
        part = pl.ds(lo, count)

        def to_group(k):
            h = lax.rem(g + k, groups)
            return remote(
                stage.at[h, part], red.at[slot, g, part], red_send.at[slot, k], red_recv.at[slot, g], (h, s)
            )

        def from_group(k):
            h = lax.rem(g + groups - k, groups)
            return remote(
                stage.at[h, part], red.at[slot, h, part], red_send.at[slot, k], red_recv.at[slot, h], (h, s)
            )

        for k in range(1, groups):
            to_group(k).start()
        red[slot, g, part] = stage[g, part]
        for k in range(1, groups):
            from_group(k).wait_recv()
        for k in range(1, groups):
            to_group(k).wait_send()
        return jnp.sum(red[slot, :, part, :], axis=0)

    def send_rows(slot):
        return [
            remote(r_send.at[slot], r_recv.at[slot, 0], r_ssem.at[slot, 0], r_rsem.at[slot, 0], (g, nxt)),
            remote(r_send.at[slot], r_recv.at[slot, 1], r_ssem.at[slot, 1], r_rsem.at[slot, 1], (g, prv)),
        ]

    def coarse_round(slot, values, stat, share, hook=None):
        hi, lo = split(values)
        both = dot(wave_t[...], hi)
        gath[slot, s, :waves, :] = both[:waves] + both[waves:] + dot(wave_t[:waves, :], lo)
        gath[slot, s, waves:, :] = jnp.zeros((STAT, columns), f32) if stat is None else stat
        if share:
            r_send[slot] = hi

        exchange(slot, 0, waves + STAT, hook)
        if share:
            for copy in send_rows(slot):
                copy.start()
        blocks = gath[slot]
        c_hi, c_lo = split(blocks[:, :waves, :].reshape(members * waves, columns))
        terms = dot(tile_hi[...], c_hi) + dot(tile_lo[...], c_hi) + dot(tile_hi[...], c_lo)
        group_stat = jnp.sum(blocks[:, waves:, :], axis=0)
        for h in range(groups):
            stage[h, :span, :] = terms[h * span : (h + 1) * span]
            stage[h, span:, :] = group_stat
        total = reduce_groups(slot, 0, span + STAT)
        if share:
            for copy in send_rows(slot):
                copy.wait()
        coarse = [total[k * waves : (k + 1) * waves] for k in range(3)]
        return coarse, jnp.sum(total[span:], axis=0, keepdims=True)

    def first_hook():
        for copy in send_t:
            copy.wait()
        for h in range(groups):
            for k, source in enumerate((tile_nb.at[0], tile, tile_nb.at[1])):
                hi, lo = split(source[h * waves : (h + 1) * waves, :])
                tile_hi[h * span + k * waves : h * span + (k + 1) * waves, :] = hi
                tile_lo[h * span + k * waves : h * span + (k + 1) * waves, :] = lo
        load_d.wait()
        prepare(dirichlet, d_left, d_send)
        d_left[:, reach:] = dot(d_left[:, reach:], flip).astype(bf16)
        for copy in send_w:
            copy.wait()
        for k in range(3):
            stack_waves(k)

    coarse, _ = coarse_round(0, rhs, None, False, first_hook)
    for k in range(3):
        lifted = lift(k, coarse[k])
        set_x(k, lifted)
        if k == 1:
            dual_ref[...] = lifted
    send_n.wait()
    send_d.start()
    residual = res3[1] - product(n_left, n_right)
    res3[1] = residual

    coarse_res, _ = coarse_round(1, residual, None, True)
    res3[0] = r_recv[1, 0].astype(f32)
    res3[2] = r_recv[1, 1].astype(f32)
    rho_prev = None
    slot = 0
    for step in range(ITERS):
        for k in range(3):
            projected = res3[k] - lift(k, coarse_res[k])
            set_x(k, projected)
            if k == 1:
                vec[...] = projected
        if step == 0:
            send_d.wait()
        precond = product(d_left, d_right)
        coarse, rho = coarse_round(slot, precond, fold(vec[...] * precond), True)
        vec[...] = precond
        for k in range(3):
            own = vec[...] if k == 1 else r_recv[slot, k // 2].astype(f32)
            direction = own - lift(k, coarse[k])
            if step > 0:
                direction = direction + rho / rho_prev * dir3[k]
            dir3[k] = direction
            set_x(k, direction)
        slot = 1 - slot
        image = product(n_left, n_right)
        vec[...] = image
        stat = fold(dir3[1] * image)
        if step + 1 < ITERS:
            coarse, curvature = coarse_round(slot, image, stat, True)
            alpha = rho / curvature
            coarse_res = [old - alpha * new for old, new in zip(coarse_res, coarse)]
            res3[0] = res3[0] - alpha * r_recv[slot, 0].astype(f32)
            res3[2] = res3[2] - alpha * r_recv[slot, 1].astype(f32)
            res3[1] = res3[1] - alpha * vec[...]
            dual_ref[...] = dual_ref[...] + alpha * dir3[1]
        else:
            gath[slot, s, waves:, :] = stat
            exchange(slot, waves, STAT)
            group_stat = jnp.sum(gath[slot, :, waves:, :], axis=0)
            for h in range(groups):
                stage[h, span:, :] = group_stat
            alpha = rho / jnp.sum(reduce_groups(slot, span, STAT), axis=0, keepdims=True)
            dual_ref[...] = dual_ref[...] + alpha * dir3[1]
            res_ref[...] = res3[1] - alpha * vec[...]
        slot = 1 - slot
        rho_prev = rho


def shards(neumann, dirichlet, coarse_inverse, loads, iface_sizes, wave_dirs):
    width = neumann.shape[2]
    reach = width // 2
    columns = loads.shape[3]
    waves = wave_dirs.shape[2]
    groups, members = lax.axis_size("grp"), lax.axis_size("sub")
    rows, depth = coarse_inverse.shape[2:]
    span = 3 * waves
    vmem = pl.BlockSpec(memory_space=pltpu.VMEM)
    dma = pltpu.SemaphoreType.DMA
    vector = jax.ShapeDtypeStruct((reach, columns), f32)
    half_matrix = pltpu.VMEM((reach, width), bf16)
    dual, residual = pl.pallas_call(
        functools.partial(kernel, groups, members),
        out_shape=(vector, vector),
        in_specs=[
            pl.BlockSpec(memory_space=pltpu.SMEM), vmem, vmem, pl.BlockSpec(memory_space=pl.ANY), vmem, vmem,
        ],
        out_specs=(vmem, vmem),
        scratch_shapes=[
            pltpu.VMEM((width, width), bf16),
            half_matrix, half_matrix, half_matrix, half_matrix, half_matrix, half_matrix,
            pltpu.VMEM((reach, columns), f32),
            pltpu.VMEM((reach, columns), f32),
            pltpu.VMEM((2, rows, depth), f32),
            pltpu.VMEM((groups * span, depth), bf16),
            pltpu.VMEM((groups * span, depth), bf16),
            pltpu.VMEM((3, waves, reach), f32),
            pltpu.VMEM((3, reach, pl.cdiv(span, 128) * 128), bf16),
            pltpu.VMEM((2 * waves, reach), bf16),
            pltpu.VMEM((2, members, waves + STAT, columns), f32),
            pltpu.VMEM((groups, span + STAT, columns), f32),
            pltpu.VMEM((2, groups, span + STAT, columns), f32),
            pltpu.VMEM((2, reach, columns), bf16),
            pltpu.VMEM((2, 2, reach, columns), bf16),
            pltpu.VMEM((3, reach, columns), f32),
            pltpu.VMEM((3, reach, columns), f32),
            pltpu.VMEM((reach, columns), f32),
            pltpu.VMEM((width, columns), bf16),
            pltpu.VMEM((width, columns), bf16),
            dma,
            dma((7,)),
            dma((7,)),
            dma((2, members // 2)),
            dma((2, members // 2)),
            dma((2, members)),
            dma((2, groups)),
            dma((2, groups)),
            dma((2, 2)),
            dma((2, 2)),
        ],
        compiler_params=pltpu.CompilerParams(
            collective_id=0, has_side_effects=True, vmem_limit_bytes=56 * 1024 * 1024
        ),
        cost_estimate=pl.CostEstimate(
            flops=14 * width * width * columns, bytes_accessed=5 * width * width, transcendentals=0
        ),
        name="dual_iterations",
    )(iface_sizes, wave_dirs[0], neumann[0, 0], dirichlet[0, 0], loads[0, 0], coarse_inverse[0, 0])
    return (dual[None, None], residual[None, None])


def solution(mesh):
    return jax.shard_map(
        shards,
        mesh=mesh,
        in_specs=(
            P("grp", "sub", None, None),
            P("grp", "sub", None, None),
            P("grp", "sub", None, None),
            P("grp", "sub", None, None),
            P("grp", "sub"),
            P("grp", "sub", None),
        ),
        out_specs=(P("grp", "sub", None, None), P("grp", "sub", None, None)),
        check_vma=False,
    )
```

time: 398 us -> 134 us (0.34)
  blocking collectives: 157 us -> 0 us
  Pallas kernels: 0 us -> 129 us
  waiting for transfers between devices: 113 us -> 0 us
  local copies, waits for them, and re-layouts: 51.6 us -> 3.74 us
  matrix products: 36.7 us -> 0 us
  other arithmetic: 17.6 us -> 0 us
  between operations: 14.7 us -> 1.29 us
  starting transfers between devices: 4.78 us -> 0 us
    pallas_call x0 -> x1, Pallas kernels: none -> 129 us  [shards(): pl.pallas_call(functools.partial(kernel, groups, members), out_shape=(vec...]
    all_gather x8 -> x0, blocking collectives: 100 us -> none  [the longest x3 43.5 us: coarse_with_stat(): lax.all_gather(coefficients(values), 'sub', axis=0, tiled=True)]
    unnamed x10 -> x0, waiting for transfers between devices: 68.7 us -> none
    ppermute x11 -> x0, waiting for transfers between devices: 43.9 us -> none  [passed_along(): return lax.ppermute(block, axis, route)]
    psum x1 -> x0, blocking collectives: 38.9 us -> none  [shards(): alpha = rho / lax.psum(jnp.sum(direction * image, axis=0), ('grp', 'sub'))]
    dot_general x21 -> x0, matrix products: 36.7 us -> none  [the longest x5 15.2 us: lift(): return jnp.dot(basis, solved, precision=highest)]
    rev x11 -> x0, local copies, waits for them, and re-layouts: 35.8 us -> none  [the longest x6 25.1 us: jump_local(): return (jnp.flip(product[width - reach:], 0) - next_head) * live[:, None]]
    unnamed x2 -> x0, blocking collectives: 17.9 us -> none
  transfers between devices with their start and end apart: 16 -> 0, of which waited for: 15 -> 0; matrix products, arithmetic and copies ran while one was open for 10% -> 0% of each run, Pallas kernels for 0% -> 0%
where the time goes in v1:
time: 134 us
  Pallas kernels  129 us (96%)
  local copies, waits for them, and re-layouts  3.74 us (3%)
    pallas_call x1, Pallas kernels, shards(): pl.pallas_call(functools.partial(kernel, groups, members), out_shape=(vec...  129 us
    unnamed x2, local copies, waits for them, and re-layouts  3.74 us

profile of v1, /device:TPU:0, one launch (start us, length us, event | category | flops | bytes accessed | tf_op | source)
XLA Modules:
  0.0 133.9 jit_solution(17124663076620610204)
XLA Ops:
  1.3 128.9 %dual_iterations.1 = (f32[512,256]{1,0:T(8,128)}, f32[512,256]{1,0:T(8,128)}) custom-call(s32[1,1]{1,0:T(1,128)S(6)} %copy.10.size_ref, s32[1,32]{1,0:T(1,128)} %bitcast.13, bf16[1024,1024]{1,0:T(8,128)(2,1)} %bitcast.9, bf16[1024,1024]{1,0:T(8,128)(2,1)} %bitcast.10, bf16[1024,256]{1,0:T(8,128)(2,1)} %bitcast.11, f32[128,256]{1,0:T(8,128)} %bitcast.12), custom_call_target="tpu_custom_call" | custom-call | flops 3758096384 | bytes 5242880 | tf_op jit(solution)/shard_map/dual_iterations/pallas_call | solution.py:327
  130.2 1.9 %copy.11 = f32[1,1,512,256]{3,2,1,0:T(8,128)} copy(f32[1,1,512,256]{3,2,1,0:T(8,128)} %bitcast.8) | data formatting | bytes 1048576
  132.1 1.9 %copy.12 = f32[1,1,512,256]{3,2,1,0:T(8,128)} copy(f32[1,1,512,256]{3,2,1,0:T(8,128)} %bitcast.7) | data formatting | bytes 1048576

commit v2 on v1

v2 whole, which is shorter than its diff:
```python
import functools

import jax
import jax.numpy as jnp
from jax import lax
from jax.experimental import pallas as pl
from jax.experimental.pallas import tpu as pltpu
from jax.sharding import PartitionSpec as P

NDIR = 64
ITERS = 2
WAVE_NUMBER = 0.785
STAT = 8
PIPES = 2
MESH = pl.DeviceIdType.MESH
f32, bf16 = jnp.float32, jnp.bfloat16


def dot(a, b):
    return jnp.dot(a, b, preferred_element_type=f32)


def split(values):
    high = values.astype(bf16)
    return high, (values - high.astype(f32)).astype(bf16)


def kernel(
    groups, members, size_ref, dirs_ref, neumann, dirichlet_hbm, loads, tile,
    dual_ref, res_ref,
    dirichlet, n_left, n_right, d_left, d_right, n_send, d_send,
    u_send, u_recv, tile_nb, tile_hi, tile_lo, bases, wave_cat, wave_t,
    gath, stage, red, r_send, r_recv,
    res3, dir3, vec, first, x_left, x_right,
    load_sem, set_send, set_recv, g_send, f_send, g_recv, red_send, red_recv, r_ssem, r_rsem,
):
    reach = n_left.shape[0]
    columns = loads.shape[1]
    waves = dirs_ref.shape[1]
    span = 3 * waves
    half = members // 2
    g, s = lax.axis_index("grp"), lax.axis_index("sub")
    nxt, prv = lax.rem(s + 1, members), lax.rem(s + members - 1, members)
    partner = s + 1 - 2 * lax.rem(s, 2)

    def remote(src, dst, send, recv, to):
        return pltpu.make_async_remote_copy(
            src_ref=src, dst_ref=dst, send_sem=send, recv_sem=recv, device_id=to, device_id_type=MESH
        )

    load_d = pltpu.make_async_copy(dirichlet_hbm, dirichlet, load_sem)
    load_d.start()

    barrier = pltpu.get_barrier_semaphore()

    def greet_sub(k, carry):
        pl.semaphore_signal(barrier, inc=1, device_id=(g, lax.rem(s + k, members)), device_id_type=MESH)
        return carry

    lax.fori_loop(1, members, greet_sub, 0)
    for k in range(1, groups):
        pl.semaphore_signal(barrier, inc=1, device_id=(lax.rem(g + k, groups), s), device_id_type=MESH)

    u_send[...] = dot(neumann[:reach, :], loads[...])
    pl.semaphore_wait(barrier, members - 1 + groups - 1)
    send_u = remote(u_send, u_recv, set_send.at[0], set_recv.at[0], (g, prv))
    send_u.start()
    send_t = [
        remote(tile, tile_nb.at[0], set_send.at[1], set_recv.at[1], (g, nxt)),
        remote(tile, tile_nb.at[1], set_send.at[2], set_recv.at[2], (g, prv)),
    ]

    back = (
        lax.broadcasted_iota(jnp.int32, (reach, reach), 0) + lax.broadcasted_iota(jnp.int32, (reach, reach), 1)
        == reach - 1
    )
    flip = jnp.where(back, 1.0, 0.0).astype(bf16)

    def prepare(matrix, left, outgoing):
        outgoing[:, :reach] = matrix[:reach, :reach]
        outgoing[:, reach:] = dot(matrix[:reach, reach:], flip).astype(bf16)
        left[...] = dot(flip, matrix[reach:, :]).astype(bf16)

    prepare(neumann, n_left, n_send)
    v = dot(n_left[...], loads[...])
    first[...] = v
    n_left[:, reach:] = dot(n_left[:, reach:], flip).astype(bf16)

    size = size_ref[0, 0]
    rows = lax.broadcasted_iota(jnp.int32, (waves, reach), 1)
    same = (
        lax.broadcasted_iota(jnp.int32, (waves, waves), 0) == lax.broadcasted_iota(jnp.int32, (waves, waves), 1)
    )
    dirs = jnp.sum(jnp.where(same, dirs_ref[...].astype(f32), 0.0), axis=1, keepdims=True)
    angle = 2.0 * jnp.pi * dirs / NDIR
    odd = lax.rem(lax.broadcasted_iota(jnp.int32, (waves, 1), 0), 2).astype(f32)
    basis = jnp.cos(WAVE_NUMBER * rows.astype(f32) * jnp.cos(angle) + odd * (jnp.pi / 2.0))
    basis = jnp.where(rows < size, basis, 0.0) / jnp.sqrt(f32(reach))
    high, low = split(basis)
    wave_t[:waves, :] = high
    wave_t[waves:, :] = low
    bases[1] = basis

    def stack_waves(k):
        hi, lo = split(bases[k])
        fill = jnp.zeros((wave_cat.shape[2] - span, reach), f32)
        padded = jnp.concatenate([hi.astype(f32), lo.astype(f32), hi.astype(f32), fill], axis=0)
        wave_cat[k] = padded.T.astype(bf16)

    send_w = [
        remote(bases.at[1], bases.at[0], set_send.at[3], set_recv.at[3], (g, nxt)),
        remote(bases.at[1], bases.at[2], set_send.at[4], set_recv.at[4], (g, prv)),
    ]
    send_n = remote(n_send, n_right, set_send.at[5], set_recv.at[5], (g, prv))
    send_d = remote(d_send, d_right, set_send.at[6], set_recv.at[6], (g, prv))
    send_u.wait_send()
    for copy in send_t + send_w + [send_n]:
        copy.start()

    cols = columns // PIPES
    live = lax.broadcasted_iota(jnp.int32, (reach, cols), 0) < size

    def lift(k, coarse):
        hi, lo = split(coarse)
        fill = jnp.zeros((wave_cat.shape[2] - span, cols), bf16)
        return dot(wave_cat[k], jnp.concatenate([hi, hi, lo, fill], axis=0))

    def fold(values):
        return jnp.sum(values.reshape(reach // STAT, STAT, cols), axis=0)

    def loop(low, body):
        def step(k, carry):
            body(k)
            return carry

        lax.fori_loop(low, half, step, 0, unroll=half <= 8)

    def pipeline(p):
        part_cols = slice(p * cols, (p + 1) * cols)

        def product(left, right):
            return jnp.where(live, dot(left[...], x_left[p]) + dot(right[...], x_right[p]), 0.0)

        def set_x(k, values):
            if k == 0:
                x_left[p, :reach, :] = (-values).astype(bf16)
            elif k == 1:
                own = values.astype(bf16)
                x_left[p, reach:, :] = own
                x_right[p, :reach, :] = own
            else:
                x_right[p, reach:, :] = (-values).astype(bf16)

        def exchange(slot, lo, count):
            part = pl.ds(lo, count)

            def block(owner):
                return gath.at[p, slot, owner, part]

            def send_peer(k):
                to = lax.rem(s + 2 * k, members)
                return remote(block(s), block(s), g_send.at[p, slot, k], g_recv.at[p, slot, s], (g, to))

            def relay(k):
                src = lax.rem(s + members - 2 * k, members)
                return remote(block(src), block(src), f_send.at[p, slot, k], g_recv.at[p, slot, src], (g, partner))

            def arrival(k):
                src = lax.rem(partner + members - 2 * k, members)
                return remote(block(src), block(src), f_send.at[p, slot, k], g_recv.at[p, slot, src], (g, partner))

            loop(1, lambda k: send_peer(k).start())
            relay(0).start()
            yield

            def pass_on(k):
                relay(k).wait_recv()
                relay(k).start()

            loop(1, pass_on)
            loop(0, lambda k: arrival(k).wait_recv())
            loop(1, lambda k: send_peer(k).wait_send())
            loop(0, lambda k: relay(k).wait_send())

        def reduce_groups(slot, lo, count):
            part = pl.ds(lo, count)

            def message(k, h, origin):
                return remote(
                    stage.at[p, h, part], red.at[p, slot, origin, part],
                    red_send.at[p, slot, k], red_recv.at[p, slot, origin], (h, s),
                )

            out = [message(k, lax.rem(g + k, groups), g) for k in range(1, groups)]
            into = [lax.rem(g + groups - k, groups) for k in range(1, groups)]
            for copy in out:
                copy.start()
            red[p, slot, g, part] = stage[p, g, part]
            yield
            for k, h in enumerate(into):
                message(k + 1, h, h).wait_recv()
            for copy in out:
                copy.wait_send()
            return jnp.sum(red[p, slot, :, part, :], axis=0)

        def send_rows(slot):
            return [
                remote(r_send.at[p, slot], r_recv.at[p, slot, side], r_ssem.at[p, slot, side],
                       r_rsem.at[p, slot, side], (g, to))
                for side, to in enumerate((nxt, prv))
            ]

        def coarse_round(slot, values, stat, share):
            hi, lo = split(values)
            both = dot(wave_t[...], hi)
            gath[p, slot, s, :waves, :] = both[:waves] + both[waves:] + dot(wave_t[:waves, :], lo)
            gath[p, slot, s, waves:, :] = jnp.zeros((STAT, cols), f32) if stat is None else stat
            if share:
                r_send[p, slot] = hi
            yield from exchange(slot, 0, waves + STAT)
            if share:
                for copy in send_rows(slot):
                    copy.start()
            blocks = gath[p, slot]
            c_hi, c_lo = split(blocks[:, :waves, :].reshape(members * waves, cols))
            terms = dot(tile_hi[...], c_hi) + dot(tile_lo[...], c_hi) + dot(tile_hi[...], c_lo)
            group_stat = jnp.sum(blocks[:, waves:, :], axis=0)
            for h in range(groups):
                stage[p, h, :span, :] = terms[h * span : (h + 1) * span]
                stage[p, h, span:, :] = group_stat
            total = yield from reduce_groups(slot, 0, span + STAT)
            if share:
                for copy in send_rows(slot):
                    copy.wait()
            coarse = [total[k * waves : (k + 1) * waves] for k in range(3)]
            return coarse, jnp.sum(total[span:], axis=0, keepdims=True)

        rhs = jnp.where(live, first[:, part_cols] - u_recv[:, part_cols], 0.0)
        res3[p, 1] = rhs
        coarse, _ = yield from coarse_round(0, rhs, None, False)
        for k in range(3):
            lifted = lift(k, coarse[k])
            set_x(k, lifted)
            if k == 1:
                dual_ref[:, part_cols] = lifted
        if p == 0:
            send_n.wait()
            send_d.start()
        residual = res3[p, 1] - product(n_left, n_right)
        res3[p, 1] = residual

        coarse_res, _ = yield from coarse_round(1, residual, None, True)
        res3[p, 0] = r_recv[p, 1, 0].astype(f32)
        res3[p, 2] = r_recv[p, 1, 1].astype(f32)
        rho_prev = None
        slot = 0
        for step in range(ITERS):
            for k in range(3):
                projected = res3[p, k] - lift(k, coarse_res[k])
                set_x(k, projected)
                if k == 1:
                    vec[p] = projected
            if step == 0 and p == 0:
                send_d.wait()
            precond = product(d_left, d_right)
            stat = fold(vec[p] * precond)
            vec[p] = precond
            coarse, rho = yield from coarse_round(slot, precond, stat, True)
            for k in range(3):
                own = vec[p] if k == 1 else r_recv[p, slot, k // 2].astype(f32)
                direction = own - lift(k, coarse[k])
                if step > 0:
                    direction = direction + rho / rho_prev * dir3[p, k]
                dir3[p, k] = direction
                set_x(k, direction)
            slot = 1 - slot
            image = product(n_left, n_right)
            vec[p] = image
            stat = fold(dir3[p, 1] * image)
            if step + 1 < ITERS:
                coarse, curvature = yield from coarse_round(slot, image, stat, True)
                alpha = rho / curvature
                coarse_res = [old - alpha * new for old, new in zip(coarse_res, coarse)]
                res3[p, 0] = res3[p, 0] - alpha * r_recv[p, slot, 0].astype(f32)
                res3[p, 2] = res3[p, 2] - alpha * r_recv[p, slot, 1].astype(f32)
                res3[p, 1] = res3[p, 1] - alpha * vec[p]
                dual_ref[:, part_cols] = dual_ref[:, part_cols] + alpha * dir3[p, 1]
            else:
                gath[p, slot, s, waves:, :] = stat
                yield from exchange(slot, waves, STAT)
                group_stat = jnp.sum(gath[p, slot, :, waves:, :], axis=0)
                for h in range(groups):
                    stage[p, h, span:, :] = group_stat
                total = yield from reduce_groups(slot, span, STAT)
                alpha = rho / jnp.sum(total, axis=0, keepdims=True)
                dual_ref[:, part_cols] = dual_ref[:, part_cols] + alpha * dir3[p, 1]
                res_ref[:, part_cols] = res3[p, 1] - alpha * vec[p]
            slot = 1 - slot
            rho_prev = rho

    pipes = [pipeline(p) for p in range(PIPES)]
    send_u.wait_recv()
    for pipe in pipes:
        next(pipe)

    for copy in send_t:
        copy.wait()
    for h in range(groups):
        for k, source in enumerate((tile_nb.at[0], tile, tile_nb.at[1])):
            hi, lo = split(source[h * waves : (h + 1) * waves, :])
            tile_hi[h * span + k * waves : h * span + (k + 1) * waves, :] = hi
            tile_lo[h * span + k * waves : h * span + (k + 1) * waves, :] = lo
    load_d.wait()
    prepare(dirichlet, d_left, d_send)
    d_left[:, reach:] = dot(d_left[:, reach:], flip).astype(bf16)
    for copy in send_w:
        copy.wait()
    for k in range(3):
        stack_waves(k)

    while pipes:
        for pipe in list(pipes):
            try:
                next(pipe)
            except StopIteration:
                pipes.remove(pipe)


def shards(neumann, dirichlet, coarse_inverse, loads, iface_sizes, wave_dirs):
    width = neumann.shape[2]
    reach = width // 2
    columns = loads.shape[3]
    waves = wave_dirs.shape[2]
    groups, members = lax.axis_size("grp"), lax.axis_size("sub")
    rows, depth = coarse_inverse.shape[2:]
    span = 3 * waves
    cols = columns // PIPES
    vmem = pl.BlockSpec(memory_space=pltpu.VMEM)
    dma = pltpu.SemaphoreType.DMA
    vector = jax.ShapeDtypeStruct((reach, columns), f32)
    half_matrix = pltpu.VMEM((reach, width), bf16)
    dual, residual = pl.pallas_call(
        functools.partial(kernel, groups, members),
        out_shape=(vector, vector),
        in_specs=[
            pl.BlockSpec(memory_space=pltpu.SMEM), vmem, vmem, pl.BlockSpec(memory_space=pl.ANY), vmem, vmem,
        ],
        out_specs=(vmem, vmem),
        scratch_shapes=[
            pltpu.VMEM((width, width), bf16),
            half_matrix, half_matrix, half_matrix, half_matrix, half_matrix, half_matrix,
            pltpu.VMEM((reach, columns), f32),
            pltpu.VMEM((reach, columns), f32),
            pltpu.VMEM((2, rows, depth), f32),
            pltpu.VMEM((groups * span, depth), bf16),
            pltpu.VMEM((groups * span, depth), bf16),
            pltpu.VMEM((3, waves, reach), f32),
            pltpu.VMEM((3, reach, pl.cdiv(span, 128) * 128), bf16),
            pltpu.VMEM((2 * waves, reach), bf16),
            pltpu.VMEM((PIPES, 2, members, waves + STAT, cols), f32),
            pltpu.VMEM((PIPES, groups, span + STAT, cols), f32),
            pltpu.VMEM((PIPES, 2, groups, span + STAT, cols), f32),
            pltpu.VMEM((PIPES, 2, reach, cols), bf16),
            pltpu.VMEM((PIPES, 2, 2, reach, cols), bf16),
            pltpu.VMEM((PIPES, 3, reach, cols), f32),
            pltpu.VMEM((PIPES, 3, reach, cols), f32),
            pltpu.VMEM((PIPES, reach, cols), f32),
            pltpu.VMEM((reach, columns), f32),
            pltpu.VMEM((PIPES, width, cols), bf16),
            pltpu.VMEM((PIPES, width, cols), bf16),
            dma,
            dma((7,)),
            dma((7,)),
            dma((PIPES, 2, members // 2)),
            dma((PIPES, 2, members // 2)),
            dma((PIPES, 2, members)),
            dma((PIPES, 2, groups)),
            dma((PIPES, 2, groups)),
            dma((PIPES, 2, 2)),
            dma((PIPES, 2, 2)),
        ],
        compiler_params=pltpu.CompilerParams(
            collective_id=0, has_side_effects=True, vmem_limit_bytes=56 * 1024 * 1024
        ),
        cost_estimate=pl.CostEstimate(
            flops=14 * width * width * columns, bytes_accessed=5 * width * width, transcendentals=0
        ),
        name="dual_iterations",
    )(iface_sizes, wave_dirs[0], neumann[0, 0], dirichlet[0, 0], loads[0, 0], coarse_inverse[0, 0])
    return (dual[None, None], residual[None, None])


def solution(mesh):
    return jax.shard_map(
        shards,
        mesh=mesh,
        in_specs=(
            P("grp", "sub", None, None),
            P("grp", "sub", None, None),
            P("grp", "sub", None, None),
            P("grp", "sub", None, None),
            P("grp", "sub"),
            P("grp", "sub", None),
        ),
        out_specs=(P("grp", "sub", None, None), P("grp", "sub", None, None)),
        check_vma=False,
    )
```

time: 134 us -> 122 us (0.910)
  Pallas kernels: 129 us -> 117 us
    pallas_call x1, Pallas kernels: 129 us -> 117 us  [shards(): pl.pallas_call(functools.partial(kernel, groups, members), out_shape=(vec...]
where the time goes in v2:
time: 122 us
  Pallas kernels  117 us (96%)
  local copies, waits for them, and re-layouts  3.74 us (3%)
  between operations  1.29 us (1%)
    pallas_call x1, Pallas kernels, shards(): pl.pallas_call(functools.partial(kernel, groups, members), out_shape=(vec...  117 us
    unnamed x2, local copies, waits for them, and re-layouts  3.74 us

profile of v2, /device:TPU:0, one launch (start us, length us, event | category | flops | bytes accessed | tf_op | source)
XLA Modules:
  0.0 121.9 jit_solution(9180287584467603656)
XLA Ops:
  1.3 116.9 %dual_iterations.1 = (f32[512,256]{1,0:T(8,128)}, f32[512,256]{1,0:T(8,128)}) custom-call(s32[1,1]{1,0:T(1,128)S(6)} %copy.10.size_ref, s32[1,32]{1,0:T(1,128)} %bitcast.13, bf16[1024,1024]{1,0:T(8,128)(2,1)} %bitcast.9, bf16[1024,1024]{1,0:T(8,128)(2,1)} %bitcast.10, bf16[1024,256]{1,0:T(8,128)(2,1)} %bitcast.11, f32[128,256]{1,0:T(8,128)} %bitcast.12), custom_call_target="tpu_custom_call" | custom-call | flops 3758096384 | bytes 5242880 | tf_op jit(solution)/shard_map/dual_iterations/pallas_call | solution.py:342
  118.1 1.9 %copy.11 = f32[1,1,512,256]{3,2,1,0:T(8,128)} copy(f32[1,1,512,256]{3,2,1,0:T(8,128)} %bitcast.8) | data formatting | bytes 1048576
  120.0 1.9 %copy.12 = f32[1,1,512,256]{3,2,1,0:T(8,128)} copy(f32[1,1,512,256]{3,2,1,0:T(8,128)} %bitcast.7) | data formatting | bytes 1048576

commit v3 on v2

--- a/solution.py
+++ b/solution.py
@@ -32,16 +32,14 @@
     u_send, u_recv, tile_nb, tile_hi, tile_lo, bases, wave_cat, wave_t,
     gath, stage, red, r_send, r_recv,
     res3, dir3, vec, first, x_left, x_right,
-    load_sem, set_send, set_recv, g_send, f_send, g_recv, red_send, red_recv, r_ssem, r_rsem,
+    load_sem, set_send, set_recv, g_send, g_recv, red_send, red_recv, r_ssem, r_rsem,
 ):
     reach = n_left.shape[0]
     columns = loads.shape[1]
     waves = dirs_ref.shape[1]
     span = 3 * waves
-    half = members // 2
     g, s = lax.axis_index("grp"), lax.axis_index("sub")
     nxt, prv = lax.rem(s + 1, members), lax.rem(s + members - 1, members)
-    partner = s + 1 - 2 * lax.rem(s, 2)
 
     def remote(src, dst, send, recv, to):
         return pltpu.make_async_remote_copy(
@@ -128,12 +126,12 @@
     def fold(values):
         return jnp.sum(values.reshape(reach // STAT, STAT, cols), axis=0)
 
-    def loop(low, body):
+    def loop(body):
         def step(k, carry):
             body(k)
             return carry
 
-        lax.fori_loop(low, half, step, 0, unroll=half <= 8)
+        lax.fori_loop(1, members, step, 0, unroll=members <= 8)
 
     def pipeline(p):
         part_cols = slice(p * cols, (p + 1) * cols)
@@ -158,29 +156,17 @@
                 return gath.at[p, slot, owner, part]
 
             def send_peer(k):
-                to = lax.rem(s + 2 * k, members)
+                to = lax.rem(s + k, members)
                 return remote(block(s), block(s), g_send.at[p, slot, k], g_recv.at[p, slot, s], (g, to))
 
-            def relay(k):
-                src = lax.rem(s + members - 2 * k, members)
-                return remote(block(src), block(src), f_send.at[p, slot, k], g_recv.at[p, slot, src], (g, partner))
-
             def arrival(k):
-                src = lax.rem(partner + members - 2 * k, members)
-                return remote(block(src), block(src), f_send.at[p, slot, k], g_recv.at[p, slot, src], (g, partner))
-
-            loop(1, lambda k: send_peer(k).start())
-            relay(0).start()
+                src = lax.rem(s + members - k, members)
+                return remote(block(src), block(src), g_send.at[p, slot, k], g_recv.at[p, slot, src], (g, nxt))
+
+            loop(lambda k: send_peer(k).start())
             yield
-
-            def pass_on(k):
-                relay(k).wait_recv()
-                relay(k).start()
-
-            loop(1, pass_on)
-            loop(0, lambda k: arrival(k).wait_recv())
-            loop(1, lambda k: send_peer(k).wait_send())
-            loop(0, lambda k: relay(k).wait_send())
+            loop(lambda k: arrival(k).wait_recv())
+            loop(lambda k: send_peer(k).wait_send())
 
         def reduce_groups(slot, lo, count):
             part = pl.ds(lo, count)
@@ -371,8 +357,7 @@
             dma,
             dma((7,)),
             dma((7,)),
-            dma((PIPES, 2, members // 2)),
-            dma((PIPES, 2, members // 2)),
+            dma((PIPES, 2, members)),
             dma((PIPES, 2, members)),
             dma((PIPES, 2, groups)),
             dma((PIPES, 2, groups)),

time: 122 us -> 126 us (1.033)
  Pallas kernels: 117 us -> 121 us
    pallas_call x1, Pallas kernels: 117 us -> 121 us  [shards(): pl.pallas_call(functools.partial(kernel, groups, members), out_shape=(vec...]
where the time goes in v3:
time: 126 us
  Pallas kernels  121 us (96%)
  local copies, waits for them, and re-layouts  3.74 us (3%)
  between operations  1.29 us (1%)
    pallas_call x1, Pallas kernels, shards(): pl.pallas_call(functools.partial(kernel, groups, members), out_shape=(vec...  121 us
    unnamed x2, local copies, waits for them, and re-layouts  3.74 us

profile of v3, /device:TPU:0, one launch (start us, length us, event | category | flops | bytes accessed | tf_op | source)
XLA Modules:
  0.0 126.1 jit_solution(6335076446258637833)
XLA Ops:
  1.3 121.1 %dual_iterations.1 = (f32[512,256]{1,0:T(8,128)}, f32[512,256]{1,0:T(8,128)}) custom-call(s32[1,1]{1,0:T(1,128)S(6)} %copy.10.size_ref, s32[1,32]{1,0:T(1,128)} %bitcast.13, bf16[1024,1024]{1,0:T(8,128)(2,1)} %bitcast.9, bf16[1024,1024]{1,0:T(8,128)(2,1)} %bitcast.10, bf16[1024,256]{1,0:T(8,128)(2,1)} %bitcast.11, f32[128,256]{1,0:T(8,128)} %bitcast.12), custom_call_target="tpu_custom_call" | custom-call | flops 3758096384 | bytes 5242880 | tf_op jit(solution)/shard_map/dual_iterations/pallas_call | solution.py:328
  122.4 1.9 %copy.11 = f32[1,1,512,256]{3,2,1,0:T(8,128)} copy(f32[1,1,512,256]{3,2,1,0:T(8,128)} %bitcast.8) | data formatting | bytes 1048576
  124.2 1.9 %copy.12 = f32[1,1,512,256]{3,2,1,0:T(8,128)} copy(f32[1,1,512,256]{3,2,1,0:T(8,128)} %bitcast.7) | data formatting | bytes 1048576

commit v4 on v2

--- a/solution.py
+++ b/solution.py
@@ -30,9 +30,9 @@
     dual_ref, res_ref,
     dirichlet, n_left, n_right, d_left, d_right, n_send, d_send,
     u_send, u_recv, tile_nb, tile_hi, tile_lo, bases, wave_cat, wave_t,
-    gath, stage, red, r_send, r_recv,
+    gath, stage, red, side_stage, side_red, r_send, r_recv,
     res3, dir3, vec, first, x_left, x_right,
-    load_sem, set_send, set_recv, g_send, f_send, g_recv, red_send, red_recv, r_ssem, r_rsem,
+    load_sem, set_send, set_recv, g_send, f_send, g_recv, red_send, red_recv, side_send, side_recv, s_send, r_ssem, r_rsem,
 ):
     reach = n_left.shape[0]
     columns = loads.shape[1]
@@ -182,26 +182,66 @@
             loop(1, lambda k: send_peer(k).wait_send())
             loop(0, lambda k: relay(k).wait_send())
 
-        def reduce_groups(slot, lo, count):
+        def exchange_small(slot, lo, count):
             part = pl.ds(lo, count)
 
-            def message(k, h, origin):
-                return remote(
-                    stage.at[p, h, part], red.at[p, slot, origin, part],
-                    red_send.at[p, slot, k], red_recv.at[p, slot, origin], (h, s),
-                )
-
-            out = [message(k, lax.rem(g + k, groups), g) for k in range(1, groups)]
+            def send(k):
+                to, ours = lax.rem(s + k, members), gath.at[p, slot, s, part]
+                return remote(ours, ours, s_send.at[p, k], g_recv.at[p, slot, s], (g, to))
+
+            def arrival(k):
+                src = lax.rem(s + members - k, members)
+                theirs = gath.at[p, slot, src, part]
+                return remote(theirs, theirs, s_send.at[p, k], g_recv.at[p, slot, src], (g, nxt))
+
+            def each(body):
+                def step(k, carry):
+                    body(k)
+                    return carry
+
+                lax.fori_loop(1, members, step, 0, unroll=members <= 8)
+
+            each(lambda k: send(k).start())
+            yield
+            each(lambda k: arrival(k).wait_recv())
+            each(lambda k: send(k).wait_send())
+
+        def reduce_groups(slot, lo, count, sides):
+            part = pl.ds(lo, count)
+
+            def messages(k, h, origin):
+                both = [
+                    remote(
+                        stage.at[p, h, part], red.at[p, slot, origin, part],
+                        red_send.at[p, slot, k], red_recv.at[p, slot, origin], (h, s),
+                    )
+                ]
+                if sides:
+                    both.append(
+                        remote(
+                            side_stage.at[p, h], side_red.at[p, slot, origin],
+                            side_send.at[p, slot, k], side_recv.at[p, slot, origin], (h, s),
+                        )
+                    )
+                return both
+
+            out = [copy for k in range(1, groups) for copy in messages(k, lax.rem(g + k, groups), g)]
             into = [lax.rem(g + groups - k, groups) for k in range(1, groups)]
             for copy in out:
                 copy.start()
             red[p, slot, g, part] = stage[p, g, part]
+            if sides:
+                side_red[p, slot, g] = side_stage[p, g]
             yield
             for k, h in enumerate(into):
-                message(k + 1, h, h).wait_recv()
+                for copy in messages(k + 1, h, h):
+                    copy.wait_recv()
             for copy in out:
                 copy.wait_send()
-            return jnp.sum(red[p, slot, :, part, :], axis=0)
+            total = jnp.sum(red[p, slot, :, part, :], axis=0)
+            if not sides:
+                return total
+            return total, jnp.sum(side_red[p, slot].astype(f32), axis=0)
 
         def send_rows(slot):
             return [
@@ -214,26 +254,31 @@
             hi, lo = split(values)
             both = dot(wave_t[...], hi)
             gath[p, slot, s, :waves, :] = both[:waves] + both[waves:] + dot(wave_t[:waves, :], lo)
-            gath[p, slot, s, waves:, :] = jnp.zeros((STAT, cols), f32) if stat is None else stat
+            used = waves if stat is None else waves + STAT
+            if stat is not None:
+                gath[p, slot, s, waves:, :] = stat
             if share:
                 r_send[p, slot] = hi
-            yield from exchange(slot, 0, waves + STAT)
+            yield from exchange(slot, 0, used)
             if share:
                 for copy in send_rows(slot):
                     copy.start()
-            blocks = gath[p, slot]
-            c_hi, c_lo = split(blocks[:, :waves, :].reshape(members * waves, cols))
+            c_hi, c_lo = split(gath[p, slot, :, :waves, :].reshape(members * waves, cols))
             terms = dot(tile_hi[...], c_hi) + dot(tile_lo[...], c_hi) + dot(tile_hi[...], c_lo)
-            group_stat = jnp.sum(blocks[:, waves:, :], axis=0)
+            group_stat = None if stat is None else jnp.sum(gath[p, slot, :, waves:, :], axis=0)
             for h in range(groups):
-                stage[p, h, :span, :] = terms[h * span : (h + 1) * span]
-                stage[p, h, span:, :] = group_stat
-            total = yield from reduce_groups(slot, 0, span + STAT)
+                rows = terms[h * span : (h + 1) * span]
+                stage[p, h, :waves, :] = rows[waves : 2 * waves]
+                side_stage[p, h, :waves, :] = rows[:waves].astype(bf16)
+                side_stage[p, h, waves:, :] = rows[2 * waves :].astype(bf16)
+                if stat is not None:
+                    stage[p, h, waves:, :] = group_stat
+            total, sides = yield from reduce_groups(slot, 0, used, True)
             if share:
                 for copy in send_rows(slot):
                     copy.wait()
-            coarse = [total[k * waves : (k + 1) * waves] for k in range(3)]
-            return coarse, jnp.sum(total[span:], axis=0, keepdims=True)
+            coarse = [sides[:waves], total[:waves], sides[waves:]]
+            return coarse, None if stat is None else jnp.sum(total[waves:], axis=0, keepdims=True)
 
         rhs = jnp.where(live, first[:, part_cols] - u_recv[:, part_cols], 0.0)
         res3[p, 1] = rhs
@@ -287,11 +332,11 @@
                 dual_ref[:, part_cols] = dual_ref[:, part_cols] + alpha * dir3[p, 1]
             else:
                 gath[p, slot, s, waves:, :] = stat
-                yield from exchange(slot, waves, STAT)
+                yield from exchange_small(slot, waves, STAT)
                 group_stat = jnp.sum(gath[p, slot, :, waves:, :], axis=0)
                 for h in range(groups):
-                    stage[p, h, span:, :] = group_stat
-                total = yield from reduce_groups(slot, span, STAT)
+                    stage[p, h, waves:, :] = group_stat
+                total = yield from reduce_groups(slot, waves, STAT, False)
                 alpha = rho / jnp.sum(total, axis=0, keepdims=True)
                 dual_ref[:, part_cols] = dual_ref[:, part_cols] + alpha * dir3[p, 1]
                 res_ref[:, part_cols] = res3[p, 1] - alpha * vec[p]
@@ -358,8 +403,10 @@
             pltpu.VMEM((3, reach, pl.cdiv(span, 128) * 128), bf16),
             pltpu.VMEM((2 * waves, reach), bf16),
             pltpu.VMEM((PIPES, 2, members, waves + STAT, cols), f32),
-            pltpu.VMEM((PIPES, groups, span + STAT, cols), f32),
-            pltpu.VMEM((PIPES, 2, groups, span + STAT, cols), f32),
+            pltpu.VMEM((PIPES, groups, waves + STAT, cols), f32),
+            pltpu.VMEM((PIPES, 2, groups, waves + STAT, cols), f32),
+            pltpu.VMEM((PIPES, groups, 2 * waves, cols), bf16),
+            pltpu.VMEM((PIPES, 2, groups, 2 * waves, cols), bf16),
             pltpu.VMEM((PIPES, 2, reach, cols), bf16),
             pltpu.VMEM((PIPES, 2, 2, reach, cols), bf16),
             pltpu.VMEM((PIPES, 3, reach, cols), f32),
@@ -376,6 +423,9 @@
             dma((PIPES, 2, members)),
             dma((PIPES, 2, groups)),
             dma((PIPES, 2, groups)),
+            dma((PIPES, 2, groups)),
+            dma((PIPES, 2, groups)),
+            dma((PIPES, members)),
             dma((PIPES, 2, 2)),
             dma((PIPES, 2, 2)),
         ],

time: 122 us -> 119 us (0.975)
  Pallas kernels: 117 us -> 113 us
    pallas_call x1, Pallas kernels: 117 us -> 113 us  [shards(): pl.pallas_call(functools.partial(kernel, groups, members), out_shape=(vec...]
where the time goes in v4:
time: 119 us
  Pallas kernels  113 us (95%)
  local copies, waits for them, and re-layouts  3.74 us (3%)
  between operations  1.29 us (1%)
    pallas_call x1, Pallas kernels, shards(): pl.pallas_call(functools.partial(kernel, groups, members), out_shape=(vec...  113 us
    unnamed x2, local copies, waits for them, and re-layouts  3.74 us

profile of v4, /device:TPU:0, one launch (start us, length us, event | category | flops | bytes accessed | tf_op | source)
XLA Modules:
  0.0 118.5 jit_solution(12650190085797827348)
XLA Ops:
  1.3 113.5 %dual_iterations.1 = (f32[512,256]{1,0:T(8,128)}, f32[512,256]{1,0:T(8,128)}) custom-call(s32[1,1]{1,0:T(1,128)S(6)} %copy.10.size_ref, s32[1,32]{1,0:T(1,128)} %bitcast.13, bf16[1024,1024]{1,0:T(8,128)(2,1)} %bitcast.9, bf16[1024,1024]{1,0:T(8,128)(2,1)} %bitcast.10, bf16[1024,256]{1,0:T(8,128)(2,1)} %bitcast.11, f32[128,256]{1,0:T(8,128)} %bitcast.12), custom_call_target="tpu_custom_call" | custom-call | flops 3758096384 | bytes 5242880 | tf_op jit(solution)/shard_map/dual_iterations/pallas_call | solution.py:387
  114.8 1.9 %copy.11 = f32[1,1,512,256]{3,2,1,0:T(8,128)} copy(f32[1,1,512,256]{3,2,1,0:T(8,128)} %bitcast.8) | data formatting | bytes 1048576
  116.6 1.9 %copy.12 = f32[1,1,512,256]{3,2,1,0:T(8,128)} copy(f32[1,1,512,256]{3,2,1,0:T(8,128)} %bitcast.7) | data formatting | bytes 1048576
